TPU v7x, 32 devices: a whole 2x2x4 slice. The times are simulated.
32 devices in a mesh: src: 32 (over z, y, x, core), dst: 1.
Axes of the slice: x: 2, y: 2, z: 4, core: 2. Of those that a mesh axis runs over, the one named last changes fastest.
Arguments:
- out_density: float32 [16384], P('src'), may hold values from 0.008 to 0.08
- in_density: float32 [16384], P('dst'), may hold values from 0.008 to 0.08
- retention: float32 [16384], P('src'), may hold values from 0.15 to 0.75
- demand: float32 [16384], P('src'), may hold values from 0.5 to 4
- location: int32 [16384], replicated, may hold values from 0 to 16383
- scenario_blocks: int32 [32], replicated, may hold values from 0 to 127
Outputs:
- out_fitness: float32 [16384], P('src')
- in_fitness: float32 [16384], P('dst')
- levels: float32 [16384, 32], P('src', 'dst')
Inputs may be any that keep to these rules, and one draw needn't show every extreme that they name: `scenario_blocks`: scenario k extracts the 128 firms of block index b = scenario_blocks_k, firms 128 * b to 128 * b + 127. `location`: several firms may share a map cell, and some cells hold none.
All inputs are finite; a program needn't handle non-finite values.
Results may differ from a plain program's by a relative error of at most 0.0003.
Values sent between devices are 32-bit elements; how exact they have to be, the bound alone decides.
A program may use at most 64 MiB of HBM per device.

v0:
```python
import math
import jax
import jax.numpy as jnp
from jax import lax
from jax.sharding import PartitionSpec as P

SWEEPS = 2
ITERS = 2
EXTRACT = 128
MAP_SIDE = 256
RANGE = 18
far_weight = 0.015625


def on_device(out_density, in_density, retention, demand, location, scenario_blocks):
    rows_dev = out_density.shape[0]
    cols_dev = in_density.shape[0]
    firms = rows_dev * lax.axis_size("src")
    row_start = lax.axis_index("src") * rows_dev
    col_start = lax.axis_index("dst") * cols_dev
    height = math.gcd(rows_dev, 128)
    blocks = rows_dev // height
    col_ids = col_start + jnp.arange(cols_dev, dtype=jnp.int32)
    offsets = jnp.arange(blocks, dtype=jnp.int32) * height
    src_cells = lax.dynamic_slice_in_dim(location, row_start, rows_dev)
    dst_cells = lax.dynamic_slice_in_dim(location, col_start, cols_dev)
    src_row = src_cells // MAP_SIDE
    src_col = src_cells % MAP_SIDE
    dst_row = dst_cells // MAP_SIDE
    dst_col = dst_cells % MAP_SIDE
    out_fit = jnp.sqrt(out_density)
    in_fit = jnp.sqrt(in_density)

    def pair_weight(offset):
        row_ids = row_start + offset + jnp.arange(height, dtype=jnp.int32)
        row_gap = lax.dynamic_slice_in_dim(src_row, offset, height)[:, None] - dst_row[None, :]
        col_gap = lax.dynamic_slice_in_dim(src_col, offset, height)[:, None] - dst_col[None, :]
        nearby = row_gap * row_gap + col_gap * col_gap <= RANGE * RANGE
        affinity = jnp.where(nearby, 1.0, far_weight)
        return jnp.where(row_ids[:, None] != col_ids[None, :], affinity, 0.0)

    for sweep_no in range(SWEEPS):

        def row_part(offset):
            row_fit = lax.dynamic_slice_in_dim(out_fit, offset, height)
            weight = pair_weight(offset)
            ratios = weight * in_fit[None, :] / (1.0 + row_fit[:, None] * in_fit[None, :] * weight)
            return jnp.sum(ratios, axis=1)

        row_partial = lax.map(row_part, offsets).reshape(rows_dev)
        row_total = lax.psum(row_partial, "dst")
        out_fit = firms * out_density / row_total

        def col_part(running, offset):
            row_fit = lax.dynamic_slice_in_dim(out_fit, offset, height)
            weight = pair_weight(offset)
            ratios = weight * row_fit[:, None] / (1.0 + row_fit[:, None] * in_fit[None, :] * weight)
            return (running + jnp.sum(ratios, axis=0), None)

        col_partial, _ = lax.scan(col_part, jnp.zeros((cols_dev,), jnp.float32), offsets)
        col_total = lax.psum(col_partial, "src")
        in_fit = firms * in_density / col_total
    row_scale = retention / (firms * out_density)

    def coeff_block(offset):
        row_fit = lax.dynamic_slice_in_dim(out_fit, offset, height)
        scale_part = lax.dynamic_slice_in_dim(row_scale, offset, height)
        product = row_fit[:, None] * in_fit[None, :] * pair_weight(offset)
        chance = product / (1.0 + product)
        return chance * scale_part[:, None]

    coefficients = lax.map(coeff_block, offsets).reshape(rows_dev, cols_dev)
    scenarios = scenario_blocks.shape[0]
    portion = scenarios // lax.axis_size("dst")
    leading = lax.axis_index("dst") * portion
    firm_rows = row_start + jnp.arange(rows_dev, dtype=jnp.int32)
    retained = (firm_rows[:, None] // EXTRACT != scenario_blocks[None, :]).astype(jnp.float32)
    levels = retained * demand[:, None]
    for round_no in range(ITERS):
        every_row = lax.all_gather(levels, "src", axis=0, tiled=True)
        columns = lax.dynamic_slice_in_dim(every_row, col_start, cols_dev, 0)
        summed = lax.psum(
            jnp.dot(
                coefficients,
                columns,
                preferred_element_type=jnp.float32,
                precision=lax.Precision.HIGHEST,
            ),
            "dst",
        )
        levels = retained * (demand[:, None] + summed)
    result = lax.dynamic_slice_in_dim(levels, leading, portion, 1)
    return (out_fit, in_fit, result)


def solution(mesh):
    in_specs = (P("src"), P("dst"), P("src"), P("src"), P(), P())
    out_specs = (P("src"), P("dst"), P("src", "dst"))
    return jax.shard_map(
        on_device, mesh=mesh, in_specs=in_specs, out_specs=out_specs, check_vma=False
    )
```

profile of v0, /device:TPU:0, one launch (start us, length us, event | category | flops | bytes accessed | tf_op | source)
XLA Modules:
  0.0 580.2 jit_solution(1393125838560426272)
XLA Ops:
  7.3 0.9 add_select_fusion
  8.2 0.8 add_select_fusion.3
  8.9 0.9 sqrt.6
  9.8 0.7 sqrt.7
  10.5 33.4 %while.55 = (s32[]{:T(128)}, f32[4,128]{1,0:T(4,128)S(1)}, s32[4]{0:T(128)S(1)}, s32[]{:T(128)}, s32[512]{0:T(512)S(1)}, /*index=5*/s32[16384]{0:T(1024)S(1)}, s...) while((s32[]{:T(128)}, f32[4,128]{1,0:T(4,128)S(1)}, ...), condition=%wide.region_2.3_spmd.clone, body=%wide.region_0.2_spmd.clone.sunk | while | flops 31457284 | bytes 203979 | solution.py:50
  10.5 0.6 dynamic_slice.120
  13.9 4.9 fusion.33
  18.9 0.6 dynamic_slice.120
  22.3 4.9 fusion.33
  30.6 4.9 fusion.33
  35.6 0.6 dynamic_slice.120
  39.0 4.9 fusion.33
  43.9 0.7 bitcast_divide_fusion.1
  44.6 34.3 %while.58 = (s32[]{:T(128)}, f32[16384]{0:T(1024)S(1)}, s32[4]{0:T(128)S(1)}, s32[]{:T(128)}, s32[512]{0:T(512)S(1)}, /*index=5*/s32[16384]{0:T(1024)S(1)}, s32[...) while((s32[]{:T(128)}, f32[16384]{0:T(1024)S(1)}, ...), condition=%wide.region_5.6_spmd.clone, body=%wide.region_3.5_spmd.clone.sunk | while | flops 31473796 | bytes 464593 | solution.py:60
  44.6 0.6 dynamic_slice.133
  48.0 5.1 fusion.36
  53.2 0.6 dynamic_slice.133
  56.6 5.1 fusion.36
  61.8 0.6 dynamic_slice.133
  65.2 5.1 fusion.36
  73.8 5.1 fusion.36
  79.0 0.6 copy-done.1
  79.7 120.3 %all-reduce.3.cloned.1.call-done = f32[16384]{0:T(1024)} async-done(((f32[16384]{0:T(1024)}), f32[16384]{0:T(1024)}) %all-reduce.3.cloned.1.call-update) | async-done | bytes 65552 | tf_op jit(solution)/shard_map/psum | solution.py:61
  200.0 0.9 multiply_divide_fusion.1
  200.9 33.4 %while.56 = (s32[]{:T(128)}, f32[4,128]{1,0:T(4,128)S(1)}, s32[4]{0:T(128)S(1)}, s32[]{:T(128)}, s32[512]{0:T(512)S(1)}, /*index=5*/s32[16384]{0:T(1024)S(1)}, s...) while((s32[]{:T(128)}, f32[4,128]{1,0:T(4,128)S(1)}, ...), condition=%wide.region_9.10_spmd.clone, body=%wide.region_7.9_spmd.clone.sunk | while | flops 31457284 | bytes 203979 | solution.py:50
  204.3 4.9 fusion.34
  212.7 4.9 fusion.34
  221.0 4.9 fusion.34
  229.4 4.9 fusion.34
  234.3 0.7 multiply_divide_fusion.2
  235.0 34.3 %while.59 = (s32[]{:T(128)}, f32[16384]{0:T(1024)S(1)}, s32[4]{0:T(128)S(1)}, s32[]{:T(128)}, s32[512]{0:T(512)S(1)}, /*index=5*/s32[16384]{0:T(1024)S(1)}, s32[...) while((s32[]{:T(128)}, f32[16384]{0:T(1024)S(1)}, ...), condition=%wide.region_12.13_spmd.clone, body=%wide.region_10.12_spmd.clone.sunk | while | flops 31473796 | bytes 464593 | solution.py:60
  238.4 5.1 fusion.37
  247.0 5.1 fusion.37
  255.6 5.1 fusion.37
  264.2 5.1 fusion.37
  269.4 0.6 copy-done.2
  270.1 0.7 compare_select_fusion
  271.0 117.5 %all-reduce.5.cloned.1.call-done = f32[16384]{0:T(1024)} async-done(((f32[16384]{0:T(1024)}), f32[16384]{0:T(1024)}) %all-reduce.5.cloned.1.call-update) | async-done | bytes 65552 | tf_op jit(solution)/shard_map/psum | solution.py:61
  388.5 0.9 multiply_divide_fusion
  389.4 39.0 %while.57 = (s32[]{:T(128)}, f32[4,128,16384]{2,1,0:T(8,128)}, s32[4]{0:T(128)S(1)}, f32[512]{0:T(512)S(1)}, f32[16384]{0:T(1024)S(1)}, /*index=5*/s32[]{:T(128)...) while((s32[]{:T(128)}, f32[4,128,16384]{2,1,0:T(8,128)}, ...), condition=%wide.region_15.16_spmd.clone, body=%wide.region_14.15_spmd.clone.sunk | while | flops 29360260 | bytes 8593107 | solution.py:72
  392.9 6.3 %fusion.35 = f32[4,128,16384]{2,1,0:T(8,128)} fusion(f32[4,128,16384]{2,1,0:T(8,128)} %get-tuple-element.1026, s32[]{:T(128)} %get-tuple-element.1025, f32[128]{0:T(128)S(1)} %dynamic_slice.129, s32[16384]{0:T(1024)S(1)} %get-tuple-element.1048, s32[128]{0:T(128)S(1)} %dynamic_slice.130, s32[16384]{0:T(1024)S(1)} %get-tuple-element.1046, ...), kind=kLoop, calls=%fused_computation.17.clone.1 | loop fusion | flops 29360128 | bytes 8588288 | tf_op jit(solution)/shard_map/while/body/jit(dynamic_update_index_in_dim)/dynamic_update_slice | solution.py:72
  402.6 6.2 %fusion.35 = f32[4,128,16384]{2,1,0:T(8,128)} fusion(f32[4,128,16384]{2,1,0:T(8,128)} %get-tuple-element.1026, s32[]{:T(128)} %get-tuple-element.1025, f32[128]{0:T(128)S(1)} %dynamic_slice.129, s32[16384]{0:T(1024)S(1)} %get-tuple-element.1048, s32[128]{0:T(128)S(1)} %dynamic_slice.130, s32[16384]{0:T(1024)S(1)} %get-tuple-element.1046, ...), kind=kLoop, calls=%fused_computation.17.clone.1 | loop fusion | flops 29360128 | bytes 8588288 | tf_op jit(solution)/shard_map/while/body/jit(dynamic_update_index_in_dim)/dynamic_update_slice | solution.py:72
  412.4 6.3 %fusion.35 = f32[4,128,16384]{2,1,0:T(8,128)} fusion(f32[4,128,16384]{2,1,0:T(8,128)} %get-tuple-element.1026, s32[]{:T(128)} %get-tuple-element.1025, f32[128]{0:T(128)S(1)} %dynamic_slice.129, s32[16384]{0:T(1024)S(1)} %get-tuple-element.1048, s32[128]{0:T(128)S(1)} %dynamic_slice.130, s32[16384]{0:T(1024)S(1)} %get-tuple-element.1046, ...), kind=kLoop, calls=%fused_computation.17.clone.1 | loop fusion | flops 29360128 | bytes 8588288 | tf_op jit(solution)/shard_map/while/body/jit(dynamic_update_index_in_dim)/dynamic_update_slice | solution.py:72
  422.1 6.2 %fusion.35 = f32[4,128,16384]{2,1,0:T(8,128)} fusion(f32[4,128,16384]{2,1,0:T(8,128)} %get-tuple-element.1026, s32[]{:T(128)} %get-tuple-element.1025, f32[128]{0:T(128)S(1)} %dynamic_slice.129, s32[16384]{0:T(1024)S(1)} %get-tuple-element.1048, s32[128]{0:T(128)S(1)} %dynamic_slice.130, s32[16384]{0:T(1024)S(1)} %get-tuple-element.1046, ...), kind=kLoop, calls=%fused_computation.17.clone.1 | loop fusion | flops 29360128 | bytes 8588288 | tf_op jit(solution)/shard_map/while/body/jit(dynamic_update_index_in_dim)/dynamic_update_slice | solution.py:72
  428.3 20.0 %all-gather.3.cloned.1.call-done = f32[16384,32]{0,1:T(8,128)} async-done(((f32[512,32]{0,1:T(8,128)}), f32[16384,32]{0,1:T(8,128)}) %all-gather.3.cloned.1.call-update) | async-done | bytes 2097168 | tf_op jit(solution)/shard_map/all_gather | solution.py:80
  448.4 35.0 %fusion.17 = f32[512,32]{0,1:T(8,128)} fusion(f32[512,16384]{1,0:T(8,128)} %bitcast.30, f32[16384,32]{0,1:T(8,128)} %all-gather.3.cloned.1.call-done, f32[512]{0:T(512)S(1)} %copy-done.4, s32[512]{0:T(512)S(1)} %add_select_fusion.2, s32[32]{0:T(128)S(1)} %copy-done.5), kind=kOutput, calls=%fused_computation.36 | convolution fusion | flops 3221274624 | bytes 35721344 | tf_op jit(solution)/shard_map/dot_general | solution.py:83
  483.4 55.3 %all-gather.5.cloned.1.call-done = f32[16384,32]{0,1:T(8,128)} async-done(((f32[512,32]{0,1:T(8,128)}), f32[16384,32]{0,1:T(8,128)}) %all-gather.5.cloned.1.call-update) | async-done | bytes 2097168 | tf_op jit(solution)/shard_map/all_gather | solution.py:80
  538.7 35.0 %fusion.16 = f32[512,32]{0,1:T(8,128)} fusion(f32[512,16384]{1,0:T(8,128)} %bitcast.31, f32[16384,32]{0,1:T(8,128)} %all-gather.5.cloned.1.call-done, f32[512]{0:T(512)S(1)} %copy-done.4, s32[512]{0:T(512)S(1)} %add_select_fusion.2, s32[32]{0:T(128)S(1)} %copy-done.5), kind=kOutput, calls=%fused_computation.34 | convolution fusion | flops 3221274624 | bytes 35721344 | tf_op jit(solution)/shard_map/dot_general | solution.py:83
  (141 shorter events, 14.0 us)
Async XLA Ops:
  7.2 381.3 %copy-start.3 = (f32[16384]{0:T(1024)S(1)}, f32[16384]{0:T(1024)}, u32[]{:S(2)}) copy-start(f32[16384]{0:T(1024)} %param.17) | copy-start | bytes 196612
  7.2 262.9 %copy-start.4 = (f32[512]{0:T(512)S(1)}, f32[512]{0:T(512)}, u32[]{:S(2)}) copy-start(f32[512]{0:T(512)} %param.19) | copy-start | bytes 6148
  7.2 262.9 %copy-start.5 = (s32[32]{0:T(128)S(1)}, s32[32]{0:T(128)}, u32[]{:S(2)}) copy-start(s32[32]{0:T(128)} %param.21) | copy-start | bytes 388
  7.2 192.8 %all-reduce.3.cloned.1.call-start = ((), (), s32[]{:S(2)}) async-start(), calls=%async_computation | async-start | bytes 131072 | tf_op jit(solution)/shard_map/psum | solution.py:61
  78.9 0.6 copy-start.1
  79.6 308.9 %all-reduce.5.cloned.1.call-start = ((), (), s32[]{:S(2)}) async-start(), calls=%async_computation.1 | async-start | bytes 131072 | tf_op jit(solution)/shard_map/psum | solution.py:61
  269.4 0.6 copy-start.2
  270.0 178.4 %all-gather.3.cloned.1.call-start = ((), (), s32[]{:S(2)}) async-start(), calls=%async_computation.2 | async-start | bytes 2162688 | tf_op jit(solution)/shard_map/all_gather | solution.py:80
  270.8 267.9 %all-gather.5.cloned.1.call-start = ((), (), s32[]{:S(2)}) async-start(), calls=%async_computation.3 | async-start | bytes 2162688 | tf_op jit(solution)/shard_map/all_gather | solution.py:80
  428.3 55.1 %copy-start = (f32[16384]{0:T(1024)}, f32[16384]{0:T(1024)S(1)}, u32[]{:S(2)}) copy-start(f32[16384]{0:T(1024)S(1)} %get-tuple-element.1067) | copy-start | bytes 196612
  428.3 55.1 %copy-start.6 = (f32[512]{0:T(512)}, f32[512]{0:T(512)S(1)}, u32[]{:S(2)}) copy-start(f32[512]{0:T(512)S(1)} %get-tuple-element.1081) | copy-start | bytes 6148
Sparse Core Ops, SparseCore 0:
  79.7 120.2 all-reduce.2
  270.1 118.3 all-reduce.4
  391.4 56.9 all-gather.2
  483.5 55.1 all-gather.4
where the time goes:
time: 581 us; the launch traced here: 580 us
  waiting for transfers between devices  313 us (54%)
  other arithmetic  111 us (19%)
  matrix products  70 us (12%)
  loops' own time  52.4 us (9%)
  local copies, waits for them, and re-layouts  19.6 us (3%)
  between operations  13.9 us (2%)
    psum x2, waiting for transfers between devices, on_device(): col_total = lax.psum(col_partial, 'src')  238 us
    all_gather x2, waiting for transfers between devices, on_device(): every_row = lax.all_gather(levels, 'src', axis=0, tiled=True)  75.3 us
    dot_general x2, matrix products, on_device(): jnp.dot(coefficients, columns, preferred_element_type=jnp.float32, precis...  70 us
    reduce_sum x8, other arithmetic, col_part(): return (running + jnp.sum(ratios, axis=0), None)  40.9 us
    reduce_sum x8, other arithmetic, row_part(): return jnp.sum(ratios, axis=1)  39.1 us
    dynamic_update_slice x4, other arithmetic, on_device(): coefficients = lax.map(coeff_block, offsets).reshape(rows_dev, cols_dev)  25 us
    another operation x2, loops' own time, on_device(): lax.scan(col_part, jnp.zeros((cols_dev,), jnp.float32), offsets)  21.1 us
    another operation x2, loops' own time, on_device(): row_partial = lax.map(row_part, offsets).reshape(rows_dev)  20.9 us
  transfers between devices with their start and end apart: 4, of which 4 were waited for; matrix products, arithmetic and copies ran while one was open for 5% of the time, Pallas kernels for 0%

commit v1 on v0

--- a/solution.py
+++ b/solution.py
@@ -58,7 +58,7 @@
             return (running + jnp.sum(ratios, axis=0), None)
 
         col_partial, _ = lax.scan(col_part, jnp.zeros((cols_dev,), jnp.float32), offsets)
-        col_total = lax.psum(col_partial, "src")
+        col_total = jnp.sum(lax.all_gather(col_partial, "src"), axis=0)
         in_fit = firms * in_density / col_total
     row_scale = retention / (firms * out_density)
 

time: 581 us -> 455 us (0.78)
  waiting for transfers between devices: 313 us -> 186 us
    psum x2 -> x0, waiting for transfers between devices: 238 us -> none  [on_device(): col_total = lax.psum(col_partial, 'src')]
    all_gather x0 -> x2, waiting for transfers between devices: none -> 114 us  [on_device(): col_total = jnp.sum(lax.all_gather(col_partial, 'src'), axis=0)]
  transfers between devices with their start and end apart: 4 -> 4, of which waited for: 4 -> 4; matrix products, arithmetic and copies ran while one was open for 5% -> 7% of each run, Pallas kernels for 0% -> 0%
where the time goes in v1:
time: 455 us; the launch traced here: 454 us
  waiting for transfers between devices  186 us (41%)
  other arithmetic  109 us (24%)
  matrix products  70 us (15%)
  loops' own time  52.4 us (12%)
  local copies, waits for them, and re-layouts  23.1 us (5%)
  between operations  14 us (3%)
    all_gather x2, waiting for transfers between devices, on_device(): col_total = jnp.sum(lax.all_gather(col_partial, 'src'), axis=0)  114 us
    all_gather x2, waiting for transfers between devices, on_device(): every_row = lax.all_gather(levels, 'src', axis=0, tiled=True)  72.2 us
    dot_general x2, matrix products, on_device(): jnp.dot(coefficients, columns, preferred_element_type=jnp.float32, precis...  70 us
    reduce_sum x8, other arithmetic, col_part(): return (running + jnp.sum(ratios, axis=0), None)  40.8 us
    reduce_sum x8, other arithmetic, row_part(): return jnp.sum(ratios, axis=1)  39.1 us
    dynamic_update_slice x4, other arithmetic, on_device(): coefficients = lax.map(coeff_block, offsets).reshape(rows_dev, cols_dev)  25 us
    another operation x2, loops' own time, on_device(): lax.scan(col_part, jnp.zeros((cols_dev,), jnp.float32), offsets)  21.1 us
    another operation x2, loops' own time, on_device(): row_partial = lax.map(row_part, offsets).reshape(rows_dev)  20.9 us
  transfers between devices with their start and end apart: 4, of which 4 were waited for; matrix products, arithmetic and copies ran while one was open for 7% of the time, Pallas kernels for 0%

profile of v1, /device:TPU:0, one launch (start us, length us, event | category | flops | bytes accessed | tf_op | source)
XLA Modules:
  0.0 454.3 jit_solution(4716506894703659780)
XLA Ops:
  7.3 0.9 add_select_fusion
  8.2 0.8 add_select_fusion.3
  9.0 0.9 sqrt.6
  9.8 0.7 sqrt.7
  10.5 33.4 %while.55 = (s32[]{:T(128)}, f32[4,128]{1,0:T(4,128)S(1)}, s32[4]{0:T(128)S(1)}, s32[]{:T(128)}, s32[512]{0:T(512)S(1)}, /*index=5*/s32[16384]{0:T(1024)S(1)}, s...) while((s32[]{:T(128)}, f32[4,128]{1,0:T(4,128)S(1)}, ...), condition=%wide.region_2.3_spmd.clone, body=%wide.region_0.2_spmd.clone.sunk | while | flops 31457284 | bytes 203979 | solution.py:50
  10.5 0.6 dynamic_slice.120
  13.9 4.9 %fusion.33 = f32[128]{0:T(128)S(1)} fusion(f32[128]{0:T(128)S(1)} %dynamic_slice.121, f32[16384]{0:T(1024)S(1)} %get-tuple-element.889, s32[16384]{0:T(1024)S(1)} %get-tuple-element.888, s32[128]{0:T(128)S(1)} %dynamic_slice.122, s32[16384]{0:T(1024)S(1)} %get-tuple-element.886, s32[128]{0:T(128)S(1)} %dynamic_slice.123, s32[128]{0:T(128)S(1)} %iota_add_fusion.11), kind=kLoop, calls=%fused_computation.8.clone.1 | loop fusion | flops 31457152 | bytes 199168 | tf_op jit(solution)/shard_map/while/body/eval_jaxpr/reduce_sum | solution.py:48
  22.3 4.9 %fusion.33 = f32[128]{0:T(128)S(1)} fusion(f32[128]{0:T(128)S(1)} %dynamic_slice.121, f32[16384]{0:T(1024)S(1)} %get-tuple-element.889, s32[16384]{0:T(1024)S(1)} %get-tuple-element.888, s32[128]{0:T(128)S(1)} %dynamic_slice.122, s32[16384]{0:T(1024)S(1)} %get-tuple-element.886, s32[128]{0:T(128)S(1)} %dynamic_slice.123, s32[128]{0:T(128)S(1)} %iota_add_fusion.11), kind=kLoop, calls=%fused_computation.8.clone.1 | loop fusion | flops 31457152 | bytes 199168 | tf_op jit(solution)/shard_map/while/body/eval_jaxpr/reduce_sum | solution.py:48
  27.2 0.6 dynamic_slice.120
  30.6 4.9 %fusion.33 = f32[128]{0:T(128)S(1)} fusion(f32[128]{0:T(128)S(1)} %dynamic_slice.121, f32[16384]{0:T(1024)S(1)} %get-tuple-element.889, s32[16384]{0:T(1024)S(1)} %get-tuple-element.888, s32[128]{0:T(128)S(1)} %dynamic_slice.122, s32[16384]{0:T(1024)S(1)} %get-tuple-element.886, s32[128]{0:T(128)S(1)} %dynamic_slice.123, s32[128]{0:T(128)S(1)} %iota_add_fusion.11), kind=kLoop, calls=%fused_computation.8.clone.1 | loop fusion | flops 31457152 | bytes 199168 | tf_op jit(solution)/shard_map/while/body/eval_jaxpr/reduce_sum | solution.py:48
  35.6 0.6 dynamic_slice.120
  39.0 4.9 %fusion.33 = f32[128]{0:T(128)S(1)} fusion(f32[128]{0:T(128)S(1)} %dynamic_slice.121, f32[16384]{0:T(1024)S(1)} %get-tuple-element.889, s32[16384]{0:T(1024)S(1)} %get-tuple-element.888, s32[128]{0:T(128)S(1)} %dynamic_slice.122, s32[16384]{0:T(1024)S(1)} %get-tuple-element.886, s32[128]{0:T(128)S(1)} %dynamic_slice.123, s32[128]{0:T(128)S(1)} %iota_add_fusion.11), kind=kLoop, calls=%fused_computation.8.clone.1 | loop fusion | flops 31457152 | bytes 199168 | tf_op jit(solution)/shard_map/while/body/eval_jaxpr/reduce_sum | solution.py:48
  43.9 0.7 bitcast_divide_fusion.1
  44.6 34.3 %while.58 = (s32[]{:T(128)}, f32[16384]{0:T(1024)S(1)}, s32[4]{0:T(128)S(1)}, s32[]{:T(128)}, s32[512]{0:T(512)S(1)}, /*index=5*/s32[16384]{0:T(1024)S(1)}, s32[...) while((s32[]{:T(128)}, f32[16384]{0:T(1024)S(1)}, ...), condition=%wide.region_5.6_spmd.clone, body=%wide.region_3.5_spmd.clone.sunk | while | flops 31473796 | bytes 464593 | solution.py:60
  44.6 0.6 dynamic_slice.133
  48.0 5.1 %fusion.36 = f32[16384]{0:T(1024)S(1)} fusion(f32[16384]{0:T(1024)S(1)} %get-tuple-element.929, f32[128]{0:T(128)S(1)} %dynamic_slice.134, s32[16384]{0:T(1024)S(1)} %get-tuple-element.927, s32[128]{0:T(128)S(1)} %dynamic_slice.135, s32[16384]{0:T(1024)S(1)} %get-tuple-element.925, s32[128]{0:T(128)S(1)} %dynamic_slice.136, s32[128]{0:T(128)S(1)} %iota_add_fusion.14), kind=kLoop, calls=%fused_computation.24.clone.1 | loop fusion | flops 31440896 | bytes 264192 | tf_op jit(solution)/shard_map/while/body/eval_jaxpr/reduce_sum | solution.py:58
  53.2 0.6 dynamic_slice.133
  56.6 5.1 %fusion.36 = f32[16384]{0:T(1024)S(1)} fusion(f32[16384]{0:T(1024)S(1)} %get-tuple-element.929, f32[128]{0:T(128)S(1)} %dynamic_slice.134, s32[16384]{0:T(1024)S(1)} %get-tuple-element.927, s32[128]{0:T(128)S(1)} %dynamic_slice.135, s32[16384]{0:T(1024)S(1)} %get-tuple-element.925, s32[128]{0:T(128)S(1)} %dynamic_slice.136, s32[128]{0:T(128)S(1)} %iota_add_fusion.14), kind=kLoop, calls=%fused_computation.24.clone.1 | loop fusion | flops 31440896 | bytes 264192 | tf_op jit(solution)/shard_map/while/body/eval_jaxpr/reduce_sum | solution.py:58
  61.7 0.6 dynamic_slice.133
  65.2 5.1 %fusion.36 = f32[16384]{0:T(1024)S(1)} fusion(f32[16384]{0:T(1024)S(1)} %get-tuple-element.929, f32[128]{0:T(128)S(1)} %dynamic_slice.134, s32[16384]{0:T(1024)S(1)} %get-tuple-element.927, s32[128]{0:T(128)S(1)} %dynamic_slice.135, s32[16384]{0:T(1024)S(1)} %get-tuple-element.925, s32[128]{0:T(128)S(1)} %dynamic_slice.136, s32[128]{0:T(128)S(1)} %iota_add_fusion.14), kind=kLoop, calls=%fused_computation.24.clone.1 | loop fusion | flops 31440896 | bytes 264192 | tf_op jit(solution)/shard_map/while/body/eval_jaxpr/reduce_sum | solution.py:58
  70.3 0.6 dynamic_slice.133
  73.7 5.1 %fusion.36 = f32[16384]{0:T(1024)S(1)} fusion(f32[16384]{0:T(1024)S(1)} %get-tuple-element.929, f32[128]{0:T(128)S(1)} %dynamic_slice.134, s32[16384]{0:T(1024)S(1)} %get-tuple-element.927, s32[128]{0:T(128)S(1)} %dynamic_slice.135, s32[16384]{0:T(1024)S(1)} %get-tuple-element.925, s32[128]{0:T(128)S(1)} %dynamic_slice.136, s32[128]{0:T(128)S(1)} %iota_add_fusion.14), kind=kLoop, calls=%fused_computation.24.clone.1 | loop fusion | flops 31440896 | bytes 264192 | tf_op jit(solution)/shard_map/while/body/eval_jaxpr/reduce_sum | solution.py:58
  78.9 0.6 copy-done.1
  79.6 59.2 %all-gather.11.cloned.1.call-done = f32[524288]{0:T(1024)} async-done(((f32[16384]{0:T(1024)}), f32[524288]{0:T(1024)}) %all-gather.11.cloned.1.call-update) | async-done | bytes 2097168 | tf_op jit(solution)/shard_map/all_gather | solution.py:61
  138.7 1.7 reshape.326
  140.8 33.4 %while.56 = (s32[]{:T(128)}, f32[4,128]{1,0:T(4,128)S(1)}, s32[4]{0:T(128)S(1)}, s32[]{:T(128)}, s32[512]{0:T(512)S(1)}, /*index=5*/s32[16384]{0:T(1024)S(1)}, s...) while((s32[]{:T(128)}, f32[4,128]{1,0:T(4,128)S(1)}, ...), condition=%wide.region_9.10_spmd.clone, body=%wide.region_7.9_spmd.clone.sunk | while | flops 31457284 | bytes 203979 | solution.py:50
  144.2 4.9 %fusion.34 = f32[128]{0:T(128)S(1)} fusion(f32[128]{0:T(128)S(1)} %dynamic_slice.125, f32[16384]{0:T(1024)S(1)} %get-tuple-element.967, s32[16384]{0:T(1024)S(1)} %get-tuple-element.966, s32[128]{0:T(128)S(1)} %dynamic_slice.126, s32[16384]{0:T(1024)S(1)} %get-tuple-element.964, s32[128]{0:T(128)S(1)} %dynamic_slice.127, s32[128]{0:T(128)S(1)} %iota_add_fusion.12), kind=kLoop, calls=%fused_computation.13.clone.1 | loop fusion | flops 31457152 | bytes 199168 | tf_op jit(solution)/shard_map/while/body/eval_jaxpr/reduce_sum | solution.py:48
  152.5 4.9 %fusion.34 = f32[128]{0:T(128)S(1)} fusion(f32[128]{0:T(128)S(1)} %dynamic_slice.125, f32[16384]{0:T(1024)S(1)} %get-tuple-element.967, s32[16384]{0:T(1024)S(1)} %get-tuple-element.966, s32[128]{0:T(128)S(1)} %dynamic_slice.126, s32[16384]{0:T(1024)S(1)} %get-tuple-element.964, s32[128]{0:T(128)S(1)} %dynamic_slice.127, s32[128]{0:T(128)S(1)} %iota_add_fusion.12), kind=kLoop, calls=%fused_computation.13.clone.1 | loop fusion | flops 31457152 | bytes 199168 | tf_op jit(solution)/shard_map/while/body/eval_jaxpr/reduce_sum | solution.py:48
  160.9 4.9 %fusion.34 = f32[128]{0:T(128)S(1)} fusion(f32[128]{0:T(128)S(1)} %dynamic_slice.125, f32[16384]{0:T(1024)S(1)} %get-tuple-element.967, s32[16384]{0:T(1024)S(1)} %get-tuple-element.966, s32[128]{0:T(128)S(1)} %dynamic_slice.126, s32[16384]{0:T(1024)S(1)} %get-tuple-element.964, s32[128]{0:T(128)S(1)} %dynamic_slice.127, s32[128]{0:T(128)S(1)} %iota_add_fusion.12), kind=kLoop, calls=%fused_computation.13.clone.1 | loop fusion | flops 31457152 | bytes 199168 | tf_op jit(solution)/shard_map/while/body/eval_jaxpr/reduce_sum | solution.py:48
  169.2 4.9 %fusion.34 = f32[128]{0:T(128)S(1)} fusion(f32[128]{0:T(128)S(1)} %dynamic_slice.125, f32[16384]{0:T(1024)S(1)} %get-tuple-element.967, s32[16384]{0:T(1024)S(1)} %get-tuple-element.966, s32[128]{0:T(128)S(1)} %dynamic_slice.126, s32[16384]{0:T(1024)S(1)} %get-tuple-element.964, s32[128]{0:T(128)S(1)} %dynamic_slice.127, s32[128]{0:T(128)S(1)} %iota_add_fusion.12), kind=kLoop, calls=%fused_computation.13.clone.1 | loop fusion | flops 31457152 | bytes 199168 | tf_op jit(solution)/shard_map/while/body/eval_jaxpr/reduce_sum | solution.py:48
  174.2 34.3 %while.59 = (s32[]{:T(128)}, f32[16384]{0:T(1024)S(1)}, s32[4]{0:T(128)S(1)}, s32[]{:T(128)}, s32[512]{0:T(512)S(1)}, /*index=5*/s32[16384]{0:T(1024)S(1)}, s32[...) while((s32[]{:T(128)}, f32[16384]{0:T(1024)S(1)}, ...), condition=%wide.region_12.13_spmd.clone, body=%wide.region_10.12_spmd.clone.sunk | while | flops 31473796 | bytes 464593 | solution.py:60
  177.6 5.1 %fusion.37 = f32[16384]{0:T(1024)S(1)} fusion(f32[16384]{0:T(1024)S(1)} %get-tuple-element.1007, f32[128]{0:T(128)S(1)} %dynamic_slice.138, s32[16384]{0:T(1024)S(1)} %get-tuple-element.1005, s32[128]{0:T(128)S(1)} %dynamic_slice.139, s32[16384]{0:T(1024)S(1)} %get-tuple-element.1003, s32[128]{0:T(128)S(1)} %dynamic_slice.140, s32[128]{0:T(128)S(1)} %iota_add_fusion.15), kind=kLoop, calls=%fused_computation.30.clone.1 | loop fusion | flops 31440896 | bytes 264192 | tf_op jit(solution)/shard_map/while/body/eval_jaxpr/reduce_sum | solution.py:58
  186.2 5.1 %fusion.37 = f32[16384]{0:T(1024)S(1)} fusion(f32[16384]{0:T(1024)S(1)} %get-tuple-element.1007, f32[128]{0:T(128)S(1)} %dynamic_slice.138, s32[16384]{0:T(1024)S(1)} %get-tuple-element.1005, s32[128]{0:T(128)S(1)} %dynamic_slice.139, s32[16384]{0:T(1024)S(1)} %get-tuple-element.1003, s32[128]{0:T(128)S(1)} %dynamic_slice.140, s32[128]{0:T(128)S(1)} %iota_add_fusion.15), kind=kLoop, calls=%fused_computation.30.clone.1 | loop fusion | flops 31440896 | bytes 264192 | tf_op jit(solution)/shard_map/while/body/eval_jaxpr/reduce_sum | solution.py:58
  194.8 5.1 %fusion.37 = f32[16384]{0:T(1024)S(1)} fusion(f32[16384]{0:T(1024)S(1)} %get-tuple-element.1007, f32[128]{0:T(128)S(1)} %dynamic_slice.138, s32[16384]{0:T(1024)S(1)} %get-tuple-element.1005, s32[128]{0:T(128)S(1)} %dynamic_slice.139, s32[16384]{0:T(1024)S(1)} %get-tuple-element.1003, s32[128]{0:T(128)S(1)} %dynamic_slice.140, s32[128]{0:T(128)S(1)} %iota_add_fusion.15), kind=kLoop, calls=%fused_computation.30.clone.1 | loop fusion | flops 31440896 | bytes 264192 | tf_op jit(solution)/shard_map/while/body/eval_jaxpr/reduce_sum | solution.py:58
  203.3 5.1 %fusion.37 = f32[16384]{0:T(1024)S(1)} fusion(f32[16384]{0:T(1024)S(1)} %get-tuple-element.1007, f32[128]{0:T(128)S(1)} %dynamic_slice.138, s32[16384]{0:T(1024)S(1)} %get-tuple-element.1005, s32[128]{0:T(128)S(1)} %dynamic_slice.139, s32[16384]{0:T(1024)S(1)} %get-tuple-element.1003, s32[128]{0:T(128)S(1)} %dynamic_slice.140, s32[128]{0:T(128)S(1)} %iota_add_fusion.15), kind=kLoop, calls=%fused_computation.30.clone.1 | loop fusion | flops 31440896 | bytes 264192 | tf_op jit(solution)/shard_map/while/body/eval_jaxpr/reduce_sum | solution.py:58
  208.5 0.6 copy-done.2
  209.2 0.7 compare_select_fusion
  210.2 54.3 %all-gather.13.cloned.1.call-done = f32[524288]{0:T(1024)} async-done(((f32[16384]{0:T(1024)}), f32[524288]{0:T(1024)}) %all-gather.13.cloned.1.call-update) | async-done | bytes 2097168 | tf_op jit(solution)/shard_map/all_gather | solution.py:61
  264.5 1.7 reshape.327
  266.5 38.9 %while.57 = (s32[]{:T(128)}, f32[4,128,16384]{2,1,0:T(8,128)}, s32[4]{0:T(128)S(1)}, f32[512]{0:T(512)S(1)}, f32[16384]{0:T(1024)S(1)}, /*index=5*/s32[]{:T(128)...) while((s32[]{:T(128)}, f32[4,128,16384]{2,1,0:T(8,128)}, ...), condition=%wide.region_15.16_spmd.clone, body=%wide.region_14.15_spmd.clone.sunk | while | flops 29360260 | bytes 8593107 | solution.py:72
  270.0 6.3 %fusion.35 = f32[4,128,16384]{2,1,0:T(8,128)} fusion(f32[4,128,16384]{2,1,0:T(8,128)} %get-tuple-element.1026, s32[]{:T(128)} %get-tuple-element.1025, f32[128]{0:T(128)S(1)} %dynamic_slice.129, s32[16384]{0:T(1024)S(1)} %get-tuple-element.1048, s32[128]{0:T(128)S(1)} %dynamic_slice.130, s32[16384]{0:T(1024)S(1)} %get-tuple-element.1046, ...), kind=kLoop, calls=%fused_computation.17.clone.1 | loop fusion | flops 29360128 | bytes 8588288 | tf_op jit(solution)/shard_map/while/body/jit(dynamic_update_index_in_dim)/dynamic_update_slice | solution.py:72
  279.8 6.2 %fusion.35 = f32[4,128,16384]{2,1,0:T(8,128)} fusion(f32[4,128,16384]{2,1,0:T(8,128)} %get-tuple-element.1026, s32[]{:T(128)} %get-tuple-element.1025, f32[128]{0:T(128)S(1)} %dynamic_slice.129, s32[16384]{0:T(1024)S(1)} %get-tuple-element.1048, s32[128]{0:T(128)S(1)} %dynamic_slice.130, s32[16384]{0:T(1024)S(1)} %get-tuple-element.1046, ...), kind=kLoop, calls=%fused_computation.17.clone.1 | loop fusion | flops 29360128 | bytes 8588288 | tf_op jit(solution)/shard_map/while/body/jit(dynamic_update_index_in_dim)/dynamic_update_slice | solution.py:72
  289.5 6.3 %fusion.35 = f32[4,128,16384]{2,1,0:T(8,128)} fusion(f32[4,128,16384]{2,1,0:T(8,128)} %get-tuple-element.1026, s32[]{:T(128)} %get-tuple-element.1025, f32[128]{0:T(128)S(1)} %dynamic_slice.129, s32[16384]{0:T(1024)S(1)} %get-tuple-element.1048, s32[128]{0:T(128)S(1)} %dynamic_slice.130, s32[16384]{0:T(1024)S(1)} %get-tuple-element.1046, ...), kind=kLoop, calls=%fused_computation.17.clone.1 | loop fusion | flops 29360128 | bytes 8588288 | tf_op jit(solution)/shard_map/while/body/jit(dynamic_update_index_in_dim)/dynamic_update_slice | solution.py:72
  299.2 6.2 %fusion.35 = f32[4,128,16384]{2,1,0:T(8,128)} fusion(f32[4,128,16384]{2,1,0:T(8,128)} %get-tuple-element.1026, s32[]{:T(128)} %get-tuple-element.1025, f32[128]{0:T(128)S(1)} %dynamic_slice.129, s32[16384]{0:T(1024)S(1)} %get-tuple-element.1048, s32[128]{0:T(128)S(1)} %dynamic_slice.130, s32[16384]{0:T(1024)S(1)} %get-tuple-element.1046, ...), kind=kLoop, calls=%fused_computation.17.clone.1 | loop fusion | flops 29360128 | bytes 8588288 | tf_op jit(solution)/shard_map/while/body/jit(dynamic_update_index_in_dim)/dynamic_update_slice | solution.py:72
  305.5 17.0 %all-gather.7.cloned.1.call-done = f32[16384,32]{0,1:T(8,128)} async-done(((f32[512,32]{0,1:T(8,128)}), f32[16384,32]{0,1:T(8,128)}) %all-gather.7.cloned.1.call-update) | async-done | bytes 2097168 | tf_op jit(solution)/shard_map/all_gather | solution.py:80
  322.4 35.0 %fusion.17 = f32[512,32]{0,1:T(8,128)} fusion(f32[512,16384]{1,0:T(8,128)} %bitcast.30, f32[16384,32]{0,1:T(8,128)} %all-gather.7.cloned.1.call-done, f32[512]{0:T(512)S(1)} %copy-done.4, s32[512]{0:T(512)S(1)} %add_select_fusion.2, s32[32]{0:T(128)S(1)} %copy-done.6), kind=kOutput, calls=%fused_computation.36 | convolution fusion | flops 3221274624 | bytes 35721344 | tf_op jit(solution)/shard_map/dot_general | solution.py:83
  357.5 55.3 %all-gather.9.cloned.1.call-done = f32[16384,32]{0,1:T(8,128)} async-done(((f32[512,32]{0,1:T(8,128)}), f32[16384,32]{0,1:T(8,128)}) %all-gather.9.cloned.1.call-update) | async-done | bytes 2097168 | tf_op jit(solution)/shard_map/all_gather | solution.py:80
  412.7 35.0 %fusion.16 = f32[512,32]{0,1:T(8,128)} fusion(f32[512,16384]{1,0:T(8,128)} %bitcast.31, f32[16384,32]{0,1:T(8,128)} %all-gather.9.cloned.1.call-done, f32[512]{0:T(512)S(1)} %copy-done.4, s32[512]{0:T(512)S(1)} %add_select_fusion.2, s32[32]{0:T(128)S(1)} %copy-done.6), kind=kOutput, calls=%fused_computation.34 | convolution fusion | flops 3221274624 | bytes 35721344 | tf_op jit(solution)/shard_map/dot_general | solution.py:83
  (149 shorter events, 13.8 us)
Async XLA Ops:
  7.2 133.5 %copy-start.3 = (f32[16384]{0:T(1024)S(1)}, f32[16384]{0:T(1024)}, u32[]{:S(2)}) copy-start(f32[16384]{0:T(1024)} %param.17) | copy-start | bytes 196612
  7.2 167.0 %copy-start.5 = (f32[512]{0:T(512)S(1)}, f32[512]{0:T(512)}, u32[]{:S(2)}) copy-start(f32[512]{0:T(512)} %param.16) | copy-start | bytes 6148
  7.2 167.0 %copy-start.7 = (f32[512]{0:T(512)S(1)}, f32[512]{0:T(512)}, u32[]{:S(2)}) copy-start(f32[512]{0:T(512)} %param.18) | copy-start | bytes 6148
  7.2 202.0 %copy-start.4 = (f32[512]{0:T(512)S(1)}, f32[512]{0:T(512)}, u32[]{:S(2)}) copy-start(f32[512]{0:T(512)} %param.19) | copy-start | bytes 6148
  7.2 202.0 %copy-start.6 = (s32[32]{0:T(128)S(1)}, s32[32]{0:T(128)}, u32[]{:S(2)}) copy-start(s32[32]{0:T(128)} %param.21) | copy-start | bytes 388
  7.2 131.5 %all-gather.11.cloned.1.call-start = ((), (), s32[]{:S(2)}) async-start(), calls=%async_computation.2 | async-start | bytes 2162688 | tf_op jit(solution)/shard_map/all_gather | solution.py:61
  78.9 0.6 copy-start.1
  79.5 185.0 %all-gather.13.cloned.1.call-start = ((), (), s32[]{:S(2)}) async-start(), calls=%async_computation.3 | async-start | bytes 2162688 | tf_op jit(solution)/shard_map/all_gather | solution.py:61
  208.5 0.6 copy-start.2
  209.1 113.3 %all-gather.7.cloned.1.call-start = ((), (), s32[]{:S(2)}) async-start(), calls=%async_computation | async-start | bytes 2162688 | tf_op jit(solution)/shard_map/all_gather | solution.py:80
  209.9 202.8 %all-gather.9.cloned.1.call-start = ((), (), s32[]{:S(2)}) async-start(), calls=%async_computation.1 | async-start | bytes 2162688 | tf_op jit(solution)/shard_map/all_gather | solution.py:80
  305.5 52.0 %copy-start = (f32[16384]{0:T(1024)}, f32[16384]{0:T(1024)S(1)}, u32[]{:S(2)}) copy-start(f32[16384]{0:T(1024)S(1)} %get-tuple-element.1067) | copy-start | bytes 196612
  305.5 52.0 %copy-start.8 = (f32[512]{0:T(512)}, f32[512]{0:T(512)S(1)}, u32[]{:S(2)}) copy-start(f32[512]{0:T(512)S(1)} %get-tuple-element.1081) | copy-start | bytes 6148
Sparse Core Ops, SparseCore 0:
  79.6 59.0 all-gather.10
  209.3 55.2 all-gather.12
  267.4 54.9 all-gather.6
  357.6 55.1 all-gather.8
